TPU v7x, 512 devices: a whole 4x4x16 slice. The times are simulated.
512 devices in a mesh: height: 128 (over x, z_lo, y), tile: 4 (over z_hi, core).
Axes of the slice: x: 4, y: 4, z: 16 (z_hi: 2, z_lo: 8; z = z_hi * 8 + z_lo), core: 2. Of those that a mesh axis runs over, the one named last changes fastest.
Arguments:
- pulse_panels: bfloat16 [128, 2, 8, 12288], P('height', None, None, 'tile'), may hold values from -6 to 6
- interp_weights: bfloat16 [128, 4, 16, 3, 128, 128], P('height', None, 'tile'), may hold values from -0.3125 to 0.3125
- range_blocks: int32 [128, 4, 16, 3], P('height', None, 'tile'), may hold values from 0 to 25
- sector_of_panel: int32 [128], replicated, may hold values from 0 to 3
- layer_cos: float32 [512, 128, 8], P('height'), may hold values from -1 to 1, as said below
- layer_sin: float32 [512, 128, 8], P('height'), may hold values from -1 to 1
- ground_cos: bfloat16 [128, 8, 2048], P(None, None, 'tile'), may hold values from -1 to 1, as said below
- ground_sin: bfloat16 [128, 8, 2048], P(None, None, 'tile'), may hold values from -1 to 1
- height_kernel: float32 [5], replicated, may hold values from 0.2 to 1
Outputs:
- image: float32 [2, 512, 2048], P(None, 'height', 'tile')
Inputs may be any that keep to these rules, and one draw needn't show every extreme that they name: range_blocks[h, s, u, k] counts range blocks of 128 bins in the window of the tile holding subtile u, widened by one block on each side: 0 is the block just before the window. layer_cos and layer_sin are the cosine and sine of one angle. ground_cos and ground_sin are the cosine and sine of one angle.
All inputs are finite; a program needn't handle non-finite values.
Results may differ from a plain program's by a relative error of at most 0.0003.
Values may be sent and summed in bfloat16 or wider, within the bound.
A program may use at most 128 MiB of HBM per device.

v0:
```python
import math

import jax
import jax.numpy as jnp
from jax import lax
from jax.sharding import PartitionSpec as P

HIGHEST = lax.Precision.HIGHEST


def with_halo(cells, sides, width):
    for axis, dim in sides:
        count = lax.axis_size(axis)
        ends = count - 1
        head = lax.slice_in_dim(cells, 0, width, axis=dim)
        tail = lax.slice_in_dim(cells, cells.shape[dim] - width, cells.shape[dim], axis=dim)
        cells = jnp.concatenate(
            [
                lax.ppermute(tail, axis, [(i, (i + 1) % count) for i in range(ends)]),
                cells,
                lax.ppermute(head, axis, [((i + 1) % count, i) for i in range(ends)]),
            ],
            axis=dim,
        )
    return cells


def passed_along(value, axis, steps):
    count = lax.axis_size(axis)
    initial, last = (max(0, -steps), min(count, count - steps))
    return lax.ppermute(value, axis, [(source, source + steps) for source in range(initial, last)])


def rotation(cosine_table, sine_table):
    upper_half = jnp.concatenate([cosine_table, -sine_table], axis=-1)
    lower_half = jnp.concatenate([sine_table, cosine_table], axis=-1)
    return jnp.concatenate([upper_half, lower_half], axis=-2)


def select_rows(rows, indices):
    return jnp.take(rows, indices, axis=1)


def focus_block(members, weights, blocks):
    samples, sectors, cosine_layer, sine_layer, cosine_ground, sine_ground = members
    number = samples.shape[0]
    passes = samples.shape[2]
    block_range = weights.shape[3]
    panel_rows = samples.reshape(number, 2 * passes, samples.shape[3] // block_range, block_range)
    chosen_weights = jnp.take(weights, sectors, axis=0)
    chosen_blocks = jnp.take(blocks, sectors, axis=0)
    picked = jax.vmap(select_rows)(panel_rows, chosen_blocks)
    amplitude = jnp.einsum(
        "ncukr,nukrg->ncug", picked, chosen_weights, preferred_element_type=jnp.float32
    )
    amplitude = amplitude.reshape(number, 2, passes, -1)
    real_part = amplitude[:, 0]
    imag_part = amplitude[:, 1]
    phase_cos = cosine_ground.astype(jnp.float32)
    phase_sin = sine_ground.astype(jnp.float32)
    turned = jnp.concatenate(
        [
            real_part * phase_cos - imag_part * phase_sin,
            real_part * phase_sin + imag_part * phase_cos,
        ],
        axis=1,
    )
    return jnp.einsum(
        "nlc,ncg->lg",
        rotation(cosine_layer, sine_layer),
        turned,
        precision=HIGHEST,
        preferred_element_type=jnp.float32,
    )


def focus_piece(
    accumulated,
    panels,
    weights,
    blocks,
    sector_of_panel,
    layer_cos,
    layer_sin,
    ground_cos,
    ground_sin,
):
    number = panels.shape[0]
    group_size = math.gcd(number, 16)
    cosine_layer = jnp.moveaxis(layer_cos, 1, 0)
    sine_layer = jnp.moveaxis(layer_sin, 1, 0)

    def blocked(source):
        return source.reshape((number // group_size, group_size) + source.shape[1:])

    members = tuple(
        (
            blocked(source)
            for source in (
                panels,
                sector_of_panel,
                cosine_layer,
                sine_layer,
                ground_cos,
                ground_sin,
            )
        )
    )

    def advance(running, member):
        return (running + focus_block(member, weights, blocks), None)

    accumulated, _ = lax.scan(advance, accumulated, members)
    return accumulated


def local(
    pulse_panels,
    interp_weights,
    range_blocks,
    sector_of_panel,
    layer_cos,
    layer_sin,
    ground_cos,
    ground_sin,
    height_kernel,
):
    weights = interp_weights[0]
    blocks = range_blocks[0]
    layers = layer_cos.shape[0]
    ground = weights.shape[1] * weights.shape[4]
    block_range = weights.shape[3]
    kernel_taps = height_kernel.shape[0]
    margin = kernel_taps // 2
    panel_count = lax.axis_size("height")
    scaling = 1.0 / math.sqrt(layer_cos.shape[2] * panel_count)
    initial = jnp.zeros((2 * layers, ground), jnp.float32)
    extended = with_halo(pulse_panels, (("tile", 3),), block_range)
    focused = focus_piece(
        initial,
        lax.all_gather(extended, "height", axis=0, tiled=True),
        weights,
        blocks,
        sector_of_panel,
        layer_cos,
        layer_sin,
        ground_cos,
        ground_sin,
    )
    volume = focused.reshape(2, layers, ground)
    padded = jnp.pad(volume, ((0, 0), (2 * margin, 2 * margin), (0, 0)))
    partial_layers = jnp.zeros((2, layers + 2 * margin, ground), jnp.float32)
    for tap_index in range(kernel_taps):
        partial_layers = (
            partial_layers
            + height_kernel[tap_index] * padded[:, tap_index : tap_index + layers + 2 * margin]
        )
    own_layers = partial_layers[:, margin : margin + layers]
    from_below = passed_along(partial_layers[:, margin + layers :], "height", 1)
    from_above = passed_along(partial_layers[:, :margin], "height", -1)
    own_layers = own_layers.at[:, :margin].add(from_below)
    own_layers = own_layers.at[:, layers - margin :].add(from_above)
    return own_layers * scaling


def solution(mesh):
    in_specs = (
        P("height", None, None, "tile"),
        P("height", None, "tile", None, None, None),
        P("height", None, "tile", None),
        P(),
        P("height", None, None),
        P("height", None, None),
        P(None, None, "tile"),
        P(None, None, "tile"),
        P(),
    )
    out_specs = P(None, "height", "tile")
    return jax.shard_map(local, mesh=mesh, in_specs=in_specs, out_specs=out_specs, check_vma=False)
```

profile of v0, /device:TPU:8, one launch (start us, length us, event | category | flops | bytes accessed | tf_op | source)
XLA Modules:
  0.0 1203.6 jit_solution(14181428495630895347)
XLA Ops:
  7.2 1.7 collective-permute-start
  10.3 15.4 %collective-permute-done.1 = bf16[1,2,8,128]{3,2,1,0:T(8,128)(2,1)S(1)} collective-permute-done((bf16[1,2,8,128]{3,2,1,0:T(8,128)(2,1)S(1)}, bf16[1,2,8,128]{3,2,1,0:T(8,128)(2,1)S(1)}, u32[]{:S(2)}, u32[]{:S(2)}) %collective-permute-start.1) | collective-permute-done | bytes 4128 | tf_op jit(solution)/shard_map/ppermute | solution.py:21
  32.5 978.5 %all-gather.2.cloned.1.call-done = bf16[128,2,8,3328]{3,2,1,0:T(8,128)(2,1)} async-done(((bf16[1,2,8,3328]{3,2,1,0:T(8,128)(2,1)}), bf16[128,2,8,3328]{3,2,1,0:T(8,128)(2,1)}) %all-gather.2.cloned.1.call-update) | async-done | bytes 13631504 | tf_op jit(solution)/shard_map/all_gather | solution.py:141
  1011.0 167.9 %while.13 = (s32[]{:T(128)}, f32[8,512]{1,0:T(8,128)S(1)}, f32[8,16,4,8]{1,0,3,2:T(8,128)S(1)}, f32[8,16,4,8]{1,0,3,2:T(8,128)}, s32[8,16]{1,0:T(8,128)S(1)}, /*...) while((s32[]{:T(128)}, f32[8,512]{1,0:T(8,128)S(1)}, ...), condition=%wide.region_1.2_spmd.clone, body=%wide.region_0.1_spmd.clone.sunk | while | flops 117459600 | bytes 45946632 | solution.py:113
  1013.6 1.9 reshape.209
  1015.5 2.3 copy.62
  1017.8 2.7 gather_fusion.2
  1020.6 3.9 gather_fusion
  1024.6 4.2 fusion.61
  1034.6 1.9 reshape.209
  1036.5 2.3 copy.62
  1038.8 2.7 gather_fusion.2
  1041.6 3.9 gather_fusion
  1045.5 4.2 fusion.61
  1055.6 1.9 reshape.209
  1057.5 2.3 copy.62
  1059.8 2.7 gather_fusion.2
  1062.6 3.9 gather_fusion
  1066.5 4.2 fusion.61
  1074.9 1.7 constant_dynamic-slice_fusion.9
  1076.6 1.9 reshape.209
  1078.5 2.3 copy.62
  1080.8 2.7 gather_fusion.2
  1083.6 3.9 gather_fusion
  1087.5 4.2 fusion.61
  1097.6 1.9 reshape.209
  1099.5 2.3 copy.62
  1101.8 2.7 gather_fusion.2
  1104.6 3.9 gather_fusion
  1108.5 4.2 fusion.61
  1118.6 1.9 reshape.209
  1120.4 2.3 copy.62
  1122.8 2.7 gather_fusion.2
  1125.6 3.9 gather_fusion
  1129.5 4.2 fusion.61
  1139.5 1.9 reshape.209
  1141.4 2.3 copy.62
  1143.7 2.7 gather_fusion.2
  1146.5 3.9 gather_fusion
  1150.5 4.2 fusion.61
  1160.5 1.9 reshape.209
  1162.4 2.3 copy.62
  1164.7 2.7 gather_fusion.2
  1167.5 3.9 gather_fusion
  1171.5 4.2 fusion.61
  1179.0 3.2 fusion.35
  1182.2 2.4 collective-permute-start.2
  1184.6 10.2 collective-permute-start.3
  (187 shorter events, 56.0 us)
Async XLA Ops:
  6.5 1004.5 %all-gather.2.cloned.1.call-start = ((), (), s32[]{:S(2)}) async-start(), calls=%async_computation | async-start | bytes 13737984 | tf_op jit(solution)/shard_map/all_gather | solution.py:141
  7.2 3.0 collective-permute-start
  9.0 16.7 %collective-permute-start.1 = (bf16[1,2,8,128]{3,2,1,0:T(8,128)(2,1)S(1)}, bf16[1,2,8,128]{3,2,1,0:T(8,128)(2,1)S(1)}, u32[]{:S(2)}, u32[]{:S(2)}) collective-permute-start(bf16[1,2,8,128]{3,2,1,0:T(8,128)(2,1)S(1)} %get-tuple-element.162), channel_id=1, source_target_pairs={{1,0},{2,1},{3,2},{5,4},{6,5},{7,6},{9,8},{10,9},{11,10},{13,12},{... | collective-permute-start | bytes 12296 | tf_op jit(solution)/shard_map/ppermute | solution.py:21
  1011.9 8.7 copy-start
  1020.6 3.9 copy-start.1
  1032.9 8.7 copy-start
  1041.6 3.9 copy-start.1
  1053.9 8.7 copy-start
  1062.6 3.9 copy-start.1
  1074.9 8.7 copy-start
  1083.6 3.9 copy-start.1
  1095.9 8.7 copy-start
  1104.6 3.9 copy-start.1
  1116.8 8.7 copy-start
  1125.5 3.9 copy-start.1
  1137.8 8.7 copy-start
  1146.5 3.9 copy-start.1
  1158.8 8.7 copy-start
  1167.5 3.9 copy-start.1
  1182.2 12.6 %collective-permute-start.2 = (f32[2,2,512]{2,1,0:T(2,128)S(1)}, f32[2,2,512]{2,1,0:T(2,128)S(1)}, u32[]{:S(2)}, u32[]{:S(2)}) collective-permute-start(f32[2,2,512]{2,1,0:T(2,128)S(1)} %get-tuple-element.164), channel_id=1, source_target_pairs={{0,4},{4,8},{8,12},{12,16},{16,20},{20,24},{24,28},{28,32},{32,36}... | collective-permute-start | bytes 24584 | tf_op jit(solution)/shard_map/ppermute | solution.py:31
  1184.6 11.5 collective-permute-start.3
Sparse Core Ops, SparseCore 0:
  27.3 983.6 all-gather.1
where the time goes:
time: 1200 us
  waiting for transfers between devices  995 us (83%)
  local copies, waits for them, and re-layouts  131 us (11%)
  matrix products  38.9 us (3%)
  starting transfers between devices  15.6 us (1%)
  between operations  13.5 us (1%)
    all_gather x1, waiting for transfers between devices, local(): lax.all_gather(extended, 'height', axis=0, tiled=True)  979 us
    reshape x16, local copies, waits for them, and re-layouts, focus_block(): samples.reshape(number, 2 * passes, samples.shape[3] // block_range, bloc...  33.7 us
    dot_general x8, matrix products, focus_block(): jnp.einsum('ncukr,nukrg->ncug', picked, chosen_weights, preferred_element...  33.5 us
    gather x8, local copies, waits for them, and re-layouts, focus_block(): chosen_weights = jnp.take(weights, sectors, axis=0)  31.5 us
    dynamic_slice x40, local copies, waits for them, and re-layouts, focus_piece(): accumulated, _ = lax.scan(advance, accumulated, members)  29 us
  transfers between devices with their start and end apart: 5, of which 3 were waited for; matrix products, arithmetic and copies ran while one was open for 0% of the time, Pallas kernels for 0%

commit v1 on v0

v1 whole, which is shorter than its diff:
```python
import functools
import math

import jax
import jax.numpy as jnp
from jax import lax
from jax.experimental import pallas as pl
from jax.experimental.pallas import tpu as pltpu
from jax.sharding import PartitionSpec as P

MESH = pl.DeviceIdType.MESH

NX, NZ, NY, NT = 4, 8, 4, 4
NH = NX * NZ * NY
HALF = NH // 2
PART = 12
BLOCKS = 26

RA_Z, RB_Z, RC_Z = 0, 8, 16
RA_L, RA_R, RA_F0, RA_F1 = 24, 32, 40, 48
RB_L, RB_R, RB_F0, RB_F1 = 56, 64, 72, 80
RB_M = 88
RA_M, RC_Y, RC_M = 120, 121, 125
RW = 126
R_COS, R_SIN, R_BLK, R_HI, R_LO = 130, 131, 132, 133, 134
RV = 135
SA_L, SB_L = 140, 148
N_SEM = 156


def kernel(
    x_ref, w_ref, blk_ref, blk_v, sector_ref, cos_ref, sin_ref, gc_ref, gs_ref, taps_ref, out_ref,
    data, w_own, w_far, blk_far, blk_smem, cos_far, sin_far, gcos, gsin, mask, rot, vol, vol_in,
    ssem, rsem, lsem,
):
    h, t = lax.axis_index("height"), lax.axis_index("tile")
    x, z, y = lax.div(h, NZ * NY), lax.rem(lax.div(h, NY), NZ), lax.rem(h, NY)
    half, xm = lax.div(x, 2), lax.rem(x, 2)

    def place(px, pz, py):
        return ((px * NZ + pz) * NY + py, t)

    y_up, y_dn, y_far = lax.rem(y + 1, NY), lax.rem(y + 3, NY), lax.rem(y + 2, NY)
    mate = place(x + 1 - 2 * xm, z, y)
    partner = place(3 - x, z, y)
    up, dn, opposite = place(x, z, y_up), place(x, z, y_dn), place(x, z, y_far)
    z_up, z_dn = place(x, z + 1, y), place(x, z - 1, y)
    hp = partner[0]

    def other(height):
        px = lax.div(height, NZ * NY)
        return (3 - px) * (NZ * NY) + lax.rem(height, NZ * NY)

    def edge(source, target, send_id, receive_id, device):
        return pltpu.make_async_remote_copy(
            src_ref=source, dst_ref=target, send_sem=ssem.at[send_id], recv_sem=rsem.at[receive_id],
            device_id=device, device_id_type=MESH,
        )

    def send(region, number, device, send_id=None):
        edge(region, region, number if send_id is None else send_id, number, device).start()

    def got(region, number):
        edge(region, region, 0, number, mate).wait_recv()

    def sent(region, number):
        edge(region, region, number, 0, mate).wait_send()

    def part_a(zi, yi):
        return data.at[pl.ds(0, PART), :, zi, yi]

    def half_a(m, zi, yi):
        return data.at[pl.ds(0, PART), m, zi, yi]

    def part_b(m, zi, yi):
        return data.at[pl.ds(PART, PART), m, zi, yi]

    def half_b(n, m, zi, yi):
        return data.at[pl.ds(PART + n * (PART // 2), PART // 2), m, zi, yi]

    def ends(m, zi, yi):
        return data.at[pl.ds(2 * PART, 2), m, zi, yi]

    def ends_line(m, yi):
        return data.at[pl.ds(2 * PART, 2), m, :, yi]

    def ends_plane(m):
        return data.at[pl.ds(2 * PART, 2), m]

    barrier = pltpu.get_barrier_semaphore()

    def greet(device):
        pl.semaphore_signal(barrier, inc=1, device_id=device, device_id_type=MESH)

    @pl.when(t > 0)
    def _():
        greet((h, t - 1))

    @pl.when(t < NT - 1)
    def _():
        greet((h, t + 1))

    @pl.when(h > 0)
    def _():
        greet((h - 1, t))
        greet((other(h - 1), t))

    @pl.when(h < NH - 1)
    def _():
        greet((h + 1, t))
        greet((other(h + 1), t))

    for device in (mate, partner, up, dn, opposite):
        greet(device)

    @pl.loop(1, NZ)
    def _(n):
        greet(place(x, lax.rem(z + n, NZ), y))

    local = [
        pltpu.make_async_copy(w_ref, w_own, lsem.at[0]),
        pltpu.make_async_copy(gc_ref.at[pl.ds(half * HALF, HALF)], gcos, lsem.at[1]),
        pltpu.make_async_copy(gs_ref.at[pl.ds(half * HALF, HALF)], gsin, lsem.at[2]),
    ]
    for copy in local:
        copy.start()
    for b in range(2 * PART):
        lanes = slice(b * 128, (b + 1) * 128)
        data[b, xm, z, y] = jnp.concatenate([x_ref[0, :, lanes], x_ref[1, :, lanes]], axis=0)

    @pl.when(t == 0)
    def _():
        data[2 * PART + 1, xm, z, y] = jnp.zeros((16, 128), jnp.bfloat16)

    @pl.when(t == NT - 1)
    def _():
        data[2 * PART, xm, z, y] = jnp.zeros((16, 128), jnp.bfloat16)

    def flag(condition):
        return jnp.where(condition, 1, 0)

    pl.semaphore_wait(
        barrier,
        5 + (NZ - 1) + flag(t > 0) + flag(t < NT - 1) + flag(h > 0) + flag(h < NH - 1) + flag(hp > 0) + flag(hp < NH - 1),
    )

    def spread(zi):
        send(part_b(xm, zi, y), RB_M + zi * NY + y, mate)
        send(part_b(xm, zi, y), RB_L + zi, up)
        send(part_b(xm, zi, y), RB_R + zi, dn)

    def spread_a(zi):
        send(part_a(zi, y), RA_L + zi, up)
        send(part_a(zi, y), RA_R + zi, dn)

    def to_z(region, number, left_id, rightward, leftward):
        @pl.when(rightward)
        def _():
            send(region, number, z_up)

        @pl.when(leftward)
        def _():
            send(region, number, z_dn, left_id)

    send(half_a(xm, z, y), RA_M, mate)
    to_z(part_b(xm, z, y), RB_Z + z, SB_L + z, z < NZ - 1, z > 0)
    spread(z)

    @pl.when(t < NT - 1)
    def _():
        edge(data.at[2 * PART - 1, xm, z, y], data.at[2 * PART + 1, xm, z, y], R_HI, R_HI, (h, t + 1)).start()

    @pl.when(t > 0)
    def _():
        edge(data.at[0, xm, z, y], data.at[2 * PART, xm, z, y], R_LO, R_LO, (h, t - 1)).start()

    edge(cos_ref, cos_far, R_COS, R_COS, partner).start()
    edge(sin_ref, sin_far, R_SIN, R_SIN, partner).start()
    edge(blk_v, blk_far, R_BLK, R_BLK, partner).start()
    for s in range(4):
        edge(w_ref.at[s], w_far.at[s], RW + s, RW + s, partner).start()
    got(half_a(1 - xm, z, y), RA_M)
    to_z(part_a(z, y), RA_Z + z, SA_L + z, z < NZ - 1, z > 0)
    spread_a(z)

    @pl.loop(0, HALF)
    def _(n):
        sector = sector_ref[half * HALF + n]
        for s in range(4):
            one = jnp.where(sector == s, 1.0, 0.0).astype(jnp.float32)
            mask[s, n] = jnp.full((16, 128), one, jnp.float32).astype(jnp.bfloat16)

    short = jnp.minimum(z, NZ - 1 - z)

    def order(k):
        paired = k <= 2 * short
        distance = jnp.where(paired, lax.div(k + 1, 2), k - short)
        from_dn = jnp.where(paired, lax.rem(k, 2) == 1, z > NZ - 1 - z)
        zi = jnp.where(k == 0, z, jnp.where(from_dn, z - distance, z + distance))
        return zi, from_dn

    @pl.loop(1, NZ + 2)
    def _(k):
        @pl.when(k < NZ)
        def _():
            zi, from_dn = order(k)
            rightward = jnp.logical_and(from_dn, z < NZ - 1)
            leftward = jnp.logical_and(jnp.logical_not(from_dn), z > 0)
            got(part_b(xm, zi, y), RB_Z + zi)
            to_z(part_b(xm, zi, y), RB_Z + zi, SB_L + zi, rightward, leftward)
            spread(zi)
            got(part_a(zi, y), RA_Z + zi)
            to_z(part_a(zi, y), RA_Z + zi, SA_L + zi, rightward, leftward)
            spread_a(zi)

        @pl.when(k <= NZ)
        def _():
            zi, _ = order(k - 1)
            got(part_b(xm, zi, y_dn), RB_L + zi)
            send(half_b(0, xm, zi, y_dn), RB_F0 + zi, up)
            send(part_b(xm, zi, y_dn), RB_M + zi * NY + y_dn, mate)
            got(part_b(xm, zi, y_up), RB_R + zi)
            send(half_b(1, xm, zi, y_up), RB_F1 + zi, dn)
            send(part_b(xm, zi, y_up), RB_M + zi * NY + y_up, mate)
            got(part_a(zi, y_dn), RA_L + zi)
            send(half_a(0, zi, y_dn), RA_F0 + zi, up)
            got(part_a(zi, y_up), RA_R + zi)
            send(half_a(1, zi, y_up), RA_F1 + zi, dn)

        @pl.when(k >= 2)
        def _():
            zi, _ = order(k - 2)
            got(half_b(0, xm, zi, y_far), RB_F0 + zi)
            got(half_b(1, xm, zi, y_far), RB_F1 + zi)
            send(part_b(xm, zi, y_far), RB_M + zi * NY + y_far, mate)

        @pl.when(k == 2)
        def _():
            @pl.when(t > 0)
            def _():
                got(data.at[2 * PART + 1, xm, z, y], R_HI)

            @pl.when(t < NT - 1)
            def _():
                got(data.at[2 * PART, xm, z, y], R_LO)

            @pl.loop(1, NZ)
            def _(n):
                zn = lax.rem(z + n, NZ)
                send(ends(xm, z, y), RC_Z + z, place(x, zn, y), RC_Z + zn)

        @pl.when(k == 4)
        def _():
            @pl.loop(1, NZ)
            def _(n):
                zn = lax.rem(z + n, NZ)
                got(ends(xm, zn, y), RC_Z + zn)

            send(ends_line(xm, y), RC_Y + y, up, RC_Y + y_up)
            send(ends_line(xm, y), RC_Y + y, dn, RC_Y + y_dn)
            send(ends_line(xm, y), RC_Y + y, opposite, RC_Y + y_far)

        @pl.when(k == 6)
        def _():
            for yi in (y_up, y_dn, y_far):
                got(ends_line(xm, yi), RC_Y + yi)
            send(ends_plane(xm), RC_M, mate)

    got(cos_far, R_COS)
    got(sin_far, R_SIN)
    got(blk_far, R_BLK)
    blocks_in = pltpu.make_async_copy(blk_far, blk_smem, lsem.at[3])
    blocks_in.start()
    lane = lax.broadcasted_iota(jnp.int32, (NH, HALF * 16), 1)
    panel = lax.broadcasted_iota(jnp.int32, (NH, HALF * 16), 0)
    expand = (lax.shift_right_logical(lane, 4) + half * HALF == panel).astype(jnp.float32).astype(jnp.bfloat16)
    row = jnp.bitwise_and(lax.broadcasted_iota(jnp.int32, (128, HALF * 16), 0), 15)
    column = jnp.bitwise_and(lax.broadcasted_iota(jnp.int32, (128, HALF * 16), 1), 15)
    for slab, (cosine, sine) in enumerate(((cos_ref, sin_ref), (cos_far, sin_far))):
        rows = []
        for layer in range(4):
            rows += [cosine[layer], -sine[layer]]
        for layer in range(4):
            rows += [sine[layer], cosine[layer]]
        table = jnp.concatenate(rows, axis=0)
        high = table.astype(jnp.bfloat16)
        low = (table - high.astype(jnp.float32)).astype(jnp.bfloat16)
        halves = []
        for piece in (high, low):
            wide = jnp.dot(piece, expand, preferred_element_type=jnp.float32)
            wide = jnp.where(row == column, wide, 0.0)
            halves.append(jnp.sum(wide.reshape(8, 16, HALF * 16), axis=1))
        rot[slab] = jnp.concatenate(halves, axis=0).astype(jnp.bfloat16)
    blocks_in.wait()
    for copy in local:
        copy.wait()

    @pl.loop(0, NZ)
    def _(zi):
        for yi in range(NY):
            got(part_b(1 - xm, zi, yi), RB_M + zi * NY + yi)
        got(half_a(0, zi, y_far), RA_F0 + zi)
        got(half_a(1, zi, y_far), RA_F1 + zi)

    got(ends_plane(1 - xm), RC_M)
    for s in range(4):
        got(w_far.at[s], RW + s)

    def focus(slab, weights, blocks):
        vol[slab] = jnp.zeros((8, 512), jnp.float32)

        @pl.loop(0, 16)
        def _(i):
            group, u = lax.div(i, 4), lax.rem(i, 4)
            lanes = pl.ds(pl.multiple_of(u * 128, 128), 128)
            panels = pl.ds(pl.multiple_of(group * 16, 16), 16)
            pieces = []
            for s in range(4):
                chosen = mask[s, panels]
                for k in range(3):
                    place_of = lax.rem(blocks[k, s, u] + (BLOCKS - 1), BLOCKS)
                    picked = data[place_of, lax.div(group, 2), pl.ds(lax.rem(group, 2) * 4, 4)]
                    pieces.append((picked.reshape(16, 16, 128) * chosen).reshape(256, 128))
            amplitude = jnp.dot(
                jnp.concatenate(pieces, axis=1), weights[:, u].reshape(12 * 128, 128),
                preferred_element_type=jnp.float32,
            ).reshape(16, 2, 8, 128)
            re, im = amplitude[:, 0], amplitude[:, 1]
            pc = gcos[panels, :, lanes].astype(jnp.float32)
            ps = gsin[panels, :, lanes].astype(jnp.float32)
            turned = jnp.concatenate([re * pc - im * ps, re * ps + im * pc], axis=1).reshape(256, 128)
            high = turned.astype(jnp.bfloat16)
            low = (turned - high.astype(jnp.float32)).astype(jnp.bfloat16)
            rotate = rot[slab, :, pl.ds(pl.multiple_of(group * 256, 256), 256)]
            layers = jnp.dot(rotate, high, preferred_element_type=jnp.float32)
            layers = layers + jnp.dot(rotate, low, preferred_element_type=jnp.float32)
            vol[slab, :, lanes] += layers[:8] + layers[8:]

    def give(slab, slot, device):
        edge(vol.at[slab], vol_in.at[slot], RV + slot, RV + slot, device).start()

    focus(1, w_far, blk_smem)
    give(1, 0, partner)

    @pl.when(hp < NH - 1)
    def _():
        give(1, 3, (hp + 1, t))

    @pl.when(hp > 0)
    def _():
        give(1, 4, (hp - 1, t))

    focus(0, w_own, blk_ref)

    @pl.when(h < NH - 1)
    def _():
        give(0, 1, (h + 1, t))

    @pl.when(h > 0)
    def _():
        give(0, 2, (h - 1, t))

    def take(slot):
        got(vol_in.at[slot], RV + slot)

    @pl.when(h > 0)
    def _():
        take(1)
        take(3)

    @pl.when(h == 0)
    def _():
        vol_in[1] = jnp.zeros((8, 512), jnp.float32)
        vol_in[3] = jnp.zeros((8, 512), jnp.float32)

    @pl.when(h < NH - 1)
    def _():
        take(2)
        take(4)

    @pl.when(h == NH - 1)
    def _():
        vol_in[2] = jnp.zeros((8, 512), jnp.float32)
        vol_in[4] = jnp.zeros((8, 512), jnp.float32)

    take(0)
    here = vol[0] + vol_in[0]
    below = vol_in[1] + vol_in[3]
    above = vol_in[2] + vol_in[4]
    for part in range(2):
        rows = jnp.concatenate(
            [below[4 * part + 2 : 4 * part + 4], here[4 * part : 4 * part + 4], above[4 * part : 4 * part + 2]], axis=0
        )
        image = jnp.zeros((4, 512), jnp.float32)
        for j in range(5):
            image = image + taps_ref[j] * rows[j : j + 4]
        out_ref[part] = image * (1.0 / math.sqrt(8 * NH))

    @pl.loop(0, NZ)
    def _(k):
        zi, from_dn = order(k)
        own = k == 0
        rightward = jnp.logical_and(jnp.logical_or(own, from_dn), z < NZ - 1)
        leftward = jnp.logical_and(jnp.logical_or(own, jnp.logical_not(from_dn)), z > 0)

        @pl.when(rightward)
        def _():
            sent(part_b(xm, zi, y), RB_Z + zi)
            sent(part_a(zi, y), RA_Z + zi)

        @pl.when(leftward)
        def _():
            sent(part_b(xm, zi, y), SB_L + zi)
            sent(part_a(zi, y), SA_L + zi)

        for number in (RB_L, RB_R):
            sent(part_b(xm, zi, y), number + zi)
        for number in (RA_L, RA_R):
            sent(part_a(zi, y), number + zi)
        for n in range(2):
            sent(half_b(n, xm, zi, y), RB_F0 + 8 * n + zi)
            sent(half_a(n, zi, y), RA_F0 + 8 * n + zi)
        for yi in range(NY):
            sent(part_b(xm, zi, yi), RB_M + zi * NY + yi)

    sent(half_a(xm, z, y), RA_M)

    @pl.loop(1, NZ)
    def _(n):
        sent(ends(xm, z, y), RC_Z + lax.rem(z + n, NZ))

    for yi in (y_up, y_dn, y_far):
        sent(ends_line(xm, y), RC_Y + yi)
    sent(ends_plane(xm), RC_M)
    for s in range(4):
        sent(w_far.at[s], RW + s)
    sent(cos_far, R_COS)
    sent(sin_far, R_SIN)
    sent(blk_far, R_BLK)

    @pl.when(t < NT - 1)
    def _():
        sent(data.at[0, xm, z, y], R_HI)

    @pl.when(t > 0)
    def _():
        sent(data.at[0, xm, z, y], R_LO)

    sent(vol.at[0], RV)
    for slot, condition in ((1, h < NH - 1), (2, h > 0), (3, hp < NH - 1), (4, hp > 0)):

        @pl.when(condition)
        def _():
            sent(vol.at[0], RV + slot)


def local(pulse_panels, interp_weights, range_blocks, sector_of_panel, layer_cos, layer_sin, ground_cos, ground_sin, height_kernel):
    blocks = jnp.transpose(range_blocks[0], (2, 0, 1))
    vmem, smem, anywhere = (pl.BlockSpec(memory_space=space) for space in (pltpu.VMEM, pltpu.SMEM, pl.ANY))
    f32, bf16, i32 = jnp.float32, jnp.bfloat16, jnp.int32
    return pl.pallas_call(
        kernel,
        out_shape=jax.ShapeDtypeStruct((2, 4, 512), f32),
        in_specs=[vmem, anywhere, smem, vmem, smem, vmem, vmem, anywhere, anywhere, smem],
        out_specs=vmem,
        scratch_shapes=[
            pltpu.VMEM((BLOCKS, 2, NZ, NY, 16, 128), bf16),
            pltpu.VMEM((4, 4, 3, 128, 128), bf16),
            pltpu.VMEM((4, 4, 3, 128, 128), bf16),
            pltpu.VMEM((3, 4, 4), i32),
            pltpu.SMEM((3, 4, 4), i32),
            pltpu.VMEM((4, 8, NH), f32),
            pltpu.VMEM((4, 8, NH), f32),
            pltpu.VMEM((HALF, 8, 512), bf16),
            pltpu.VMEM((HALF, 8, 512), bf16),
            pltpu.VMEM((4, HALF, 16, 128), bf16),
            pltpu.VMEM((2, 16, HALF * 16), bf16),
            pltpu.VMEM((2, 8, 512), f32),
            pltpu.VMEM((5, 8, 512), f32),
            pltpu.SemaphoreType.DMA((N_SEM,)),
            pltpu.SemaphoreType.DMA((N_SEM,)),
            pltpu.SemaphoreType.DMA((4,)),
        ],
        compiler_params=pltpu.CompilerParams(collective_id=0, has_side_effects=True, vmem_limit_bytes=48 << 20),
        name="focus",
    )(
        pulse_panels[0], interp_weights[0], blocks, blocks, sector_of_panel,
        jnp.swapaxes(layer_cos, 1, 2), jnp.swapaxes(layer_sin, 1, 2), ground_cos, ground_sin, height_kernel,
    )


def solution(mesh):
    in_specs = (
        P("height", None, None, "tile"),
        P("height", None, "tile", None, None, None),
        P("height", None, "tile", None),
        P(),
        P("height", None, None),
        P("height", None, None),
        P(None, None, "tile"),
        P(None, None, "tile"),
        P(),
    )
    return jax.shard_map(local, mesh=mesh, in_specs=in_specs, out_specs=P(None, "height", "tile"), check_vma=False)
```

time: 1200 us -> 105 us (0.09)
  the two profiles are of different devices: /device:TPU:8 before, /device:TPU:6 now
where the time goes in v1:
time: 105 us
  Pallas kernels  96 us (91%)
  local copies, waits for them, and re-layouts  8.79 us (8%)
    pallas_call x1, Pallas kernels, local(): pl.pallas_call(kernel, out_shape=jax.ShapeDtypeStruct((2, 4, 512), f32),...  96 us
    unnamed x19, local copies, waits for them, and re-layouts  8.79 us

profile of v1, /device:TPU:6, one launch (start us, length us, event | category | flops | bytes accessed | tf_op | source)
XLA Modules:
  0.0 104.8 jit_solution(12908253678548116421)
XLA Ops:
  0.0 0.0 copy-start
  0.0 1.4 %copy-done = bf16[1,4,4,3,128,128]{5,4,3,2,1,0:T(8,128)(2,1)S(1)} copy-done((bf16[1,4,4,3,128,128]{5,4,3,2,1,0:T(8,128)(2,1)S(1)}, bf16[1,4,4,3,128,128]{5,4,3,2,1,0:T(8,128)(2,1)}, u32[]{:S(2)}) %copy-start) | copy-done | bytes 1572888
  1.4 0.0 copy-start.1
  1.4 1.2 %copy-done.1 = bf16[128,8,512]{2,1,0:T(8,128)(2,1)S(1)} copy-done((bf16[128,8,512]{2,1,0:T(8,128)(2,1)S(1)}, bf16[128,8,512]{2,1,0:T(8,128)(2,1)}, u32[]{:S(2)}) %copy-start.1) | copy-done | bytes 1048600
  2.6 0.0 copy-start.2
  2.6 1.2 %copy-done.2 = bf16[128,8,512]{2,1,0:T(8,128)(2,1)S(1)} copy-done((bf16[128,8,512]{2,1,0:T(8,128)(2,1)S(1)}, bf16[128,8,512]{2,1,0:T(8,128)(2,1)}, u32[]{:S(2)}) %copy-start.2) | copy-done | bytes 1048600
  3.9 0.0 copy-start.3
  3.9 0.9 copy-done.3
  4.8 0.0 copy-start.4
  4.8 0.7 copy-done.4
  5.4 0.0 copy-start.5
  5.4 0.7 copy-done.5
  6.2 0.0 copy-start.6
  6.2 0.7 copy-done.6
  6.9 0.0 copy-start.7
  6.9 0.7 copy-done.7
  7.5 0.0 copy-start.8
  7.5 0.7 copy-done.8
  8.2 96.0 %focus.1 = f32[2,4,512]{2,1,0:T(4,128)S(1)} custom-call(bf16[2,8,3072]{2,1,0:T(8,128)(2,1)S(1)} %bitcast.8, bf16[4,4,3,128,128]{4,3,2,1,0:T(8,128)(2,1)S(1)} %bitcast.7, s32[3,4,4]{2,1,0:T(4,128)S(1)} %bitcast.9, s32[3,4,4]{2,1,0:T(4,128)S(1)} %bitcast.10, s32[128]{0:T(128)S(1)} %copy-done.7, f32[4,8,128]{2,1,0:T(8,128)S(1)} %bitcast.11, ...), custom_call_target="tpu_custom_call" | custom-call | tf_op jit(solution)/shard_map/focus/pallas_call | solution.py:461
  104.2 0.6 copy.11
Async XLA Ops:
  0.0 1.4 %copy-start = (bf16[1,4,4,3,128,128]{5,4,3,2,1,0:T(8,128)(2,1)S(1)}, bf16[1,4,4,3,128,128]{5,4,3,2,1,0:T(8,128)(2,1)}, u32[]{:S(2)}) copy-start(bf16[1,4,4,3,128,128]{5,4,3,2,1,0:T(8,128)(2,1)} %param.10) | copy-start | bytes 4718596
  1.4 1.2 %copy-start.1 = (bf16[128,8,512]{2,1,0:T(8,128)(2,1)S(1)}, bf16[128,8,512]{2,1,0:T(8,128)(2,1)}, u32[]{:S(2)}) copy-start(bf16[128,8,512]{2,1,0:T(8,128)(2,1)} %gc_ref.1) | copy-start | bytes 3145732
  2.6 1.2 %copy-start.2 = (bf16[128,8,512]{2,1,0:T(8,128)(2,1)S(1)}, bf16[128,8,512]{2,1,0:T(8,128)(2,1)}, u32[]{:S(2)}) copy-start(bf16[128,8,512]{2,1,0:T(8,128)(2,1)} %gs_ref.1) | copy-start | bytes 3145732
  3.9 0.9 copy-start.3
  4.8 0.7 copy-start.4
  5.4 0.7 copy-start.5
  6.2 0.7 copy-start.6
  6.9 0.7 copy-start.7
  7.5 0.7 copy-start.8

commit v2 on v0

v2 whole, which is shorter than its diff:
```python
import math

import jax
import jax.numpy as jnp
from jax import lax
from jax.experimental import pallas as pl
from jax.experimental.pallas import tpu as pltpu
from jax.sharding import PartitionSpec as P

MESH = pl.DeviceIdType.MESH

NX, NZ, NY, NT = 4, 8, 4, 4
NH = NX * NZ * NY
HALF = NH // 2
WINDOW = 24
BLOCKS = WINDOW + 2
PART = 10
GROUPS = NZ // 2

A_MATE, B_Z, A_Z, B_DN, B_UP, B_FAR, A_DN, A_UP, ENDS, ENDS_MATE, ENDS_Z, FOCUS = range(12)
ORDER = (
    (A_MATE, 0), (B_Z, 1), (B_DN, 0), (B_UP, 0), (B_Z, 2), (ENDS, 0), (A_Z, 1), (A_DN, 0), (A_UP, 0), (B_DN, 1),
    (B_UP, 1), (B_Z, 4), (B_Z, 3), (B_FAR, 0), (A_Z, 2), (B_DN, 2), (B_UP, 2), (A_DN, 1), (A_UP, 1), (B_Z, 5),
    (B_FAR, 1), (A_Z, 3), (B_Z, 6), (B_DN, 4), (B_UP, 4), (A_Z, 4), (B_DN, 3), (B_UP, 3), (A_DN, 2), (A_UP, 2),
    (B_FAR, 2), (B_Z, 7), (ENDS_MATE, 0), (A_Z, 5), (B_DN, 5), (B_UP, 5), (A_DN, 3), (A_UP, 3), (A_Z, 6), (B_DN, 6),
    (ENDS_Z, 0), (B_UP, 6), (B_FAR, 4), (A_DN, 4), (A_UP, 4), (B_FAR, 3), (A_Z, 7), (B_DN, 7), (B_UP, 7),
    (FOCUS, 0, 0), (A_DN, 5), (A_UP, 5), (B_FAR, 5), (FOCUS, 0, 1), (A_DN, 6), (A_UP, 6), (B_FAR, 6), (FOCUS, 1, 0),
    (FOCUS, 1, 1), (A_DN, 7), (A_UP, 7), (B_FAR, 7), (FOCUS, 2, 0), (FOCUS, 2, 1), (FOCUS, 3, 1), (FOCUS, 3, 0),
)
ONWARD = {0: (4, 2, 1), 4: (2, 1), 2: (1,), 6: (1,)}
N_SEND, N_RECEIVE, N_LOCAL = 256, 224, 24


def kernel(
    x_hbm, w_ref, blk_hbm, sector_hbm, cos_hbm, sin_hbm, gc_ref, gs_ref, taps_hbm, out_ref,
    x_ref, blk_v, blk_ref, sector_ref, cos_ref, sin_ref, taps_ref, data0, data1, data2, data3,
    w_own, w_far, blk_far, blk_smem, cos_far, sin_far, gcos, gsin, mask, rot, vol, vol_in,
    ssem, rsem, lsem, ready,
):
    data = (data0, data1, data2, data3)
    h, t = lax.axis_index("height"), lax.axis_index("tile")
    x, z, y = lax.div(h, NZ * NY), lax.rem(lax.div(h, NY), NZ), lax.rem(h, NY)
    half, xm = lax.div(x, 2), lax.rem(x, 2)

    def place(px, pz, py):
        return ((px * NZ + pz) * NY + py, t)

    def z_at(distance):
        flipped = z
        for bit in (1, 2, 4):
            if distance & bit:
                flipped = flipped + bit - 2 * bit * lax.rem(lax.div(z, bit), 2)
        return flipped

    y_up, y_dn, y_far = lax.rem(y + 1, NY), lax.rem(y + 3, NY), lax.rem(y + 2, NY)
    mate = place(x + 1 - 2 * xm, z, y)
    partner = place(3 - x, z, y)
    up, dn, opposite = place(x, z, y_up), place(x, z, y_dn), place(x, z, y_far)
    along = [place(x, z_at(d), y) for d in range(NZ)]
    hp = partner[0]

    receive_ids, sends = {}, []

    def receive_id(key):
        return receive_ids.setdefault(key, len(receive_ids))

    def edge(source, target, send_id, key, device):
        return pltpu.make_async_remote_copy(
            src_ref=source, dst_ref=target, send_sem=ssem.at[send_id], recv_sem=rsem.at[receive_id(key)],
            device_id=device, device_id_type=MESH,
        )

    def send(source, key, device, target=None, condition=None):
        number = len(sends)
        sends.append((source, condition))
        copy = edge(source, source if target is None else target, number, key, device)
        if condition is None:
            copy.start()
        else:
            pl.when(condition)(copy.start)

    def got(region, key):
        edge(region, region, 0, key, mate).wait_recv()

    retired = [0, 0]

    def retire():
        for number in range(*retired):
            source, condition = sends[number]
            copy = edge(source, source, number, ("a_mate",), mate)
            if condition is None:
                copy.wait_send()
            else:
                pl.when(condition)(copy.wait_send)
        retired[:] = [retired[1], len(sends)]

    def part_a(o, yi):
        return data[o // 2].at[pl.ds(0, PART), o % 2, :, yi]

    def half_a(m, o, yi):
        return data[o // 2].at[pl.ds(0, PART), o % 2, m, yi]

    def part_b(m, o, yi):
        return data[o // 2].at[pl.ds(PART, WINDOW - PART), o % 2, m, yi]

    def half_b(n, o, yi):
        size = (WINDOW - PART) // 2
        return data[o // 2].at[pl.ds(PART + n * size, size), o % 2, xm, yi]

    def ends(o, yi):
        return data[o // 2].at[pl.ds(WINDOW, 2), o % 2, :, yi]

    def ends_all(g, yi):
        return data[g].at[pl.ds(WINDOW, 2), :, :, yi]

    def own(block):
        return data0.at[block, 0, xm, y]

    barrier = pltpu.get_barrier_semaphore()

    def greet(device):
        pl.semaphore_signal(barrier, inc=1, device_id=device, device_id_type=MESH)

    @pl.when(t > 0)
    def _():
        greet((h, t - 1))

    @pl.when(t < NT - 1)
    def _():
        greet((h, t + 1))

    near = [along[4], along[2], along[1], opposite, up, dn, mate, partner]
    for device in near:
        greet(device)

    local_copies = [
        (w_ref, w_own), (sector_hbm, sector_ref), (taps_hbm, taps_ref), (blk_hbm, blk_ref),
    ]
    for o in range(NZ):
        local_copies += [(gc_ref.at[half, :, z_at(o)], gcos.at[o]), (gs_ref.at[half, :, z_at(o)], gsin.at[o])]
    first_copies = [(x_hbm, x_ref), (blk_hbm, blk_v), (cos_hbm, cos_ref), (sin_hbm, sin_ref)]
    copies = [
        pltpu.make_async_copy(source, target, lsem.at[n]) for n, (source, target) in enumerate(first_copies + local_copies)
    ]
    for copy in copies:
        copy.start()
    for copy in copies[: len(first_copies)]:
        copy.wait()
    for b in range(WINDOW):
        lanes = slice(b * 128, (b + 1) * 128)
        data0[b, 0, xm, y] = jnp.concatenate([x_ref[0, :, lanes], x_ref[1, :, lanes]], axis=0)

    @pl.when(t == 0)
    def _():
        data0[WINDOW + 1, 0, xm, y] = jnp.zeros((16, 128), jnp.bfloat16)

    @pl.when(t == NT - 1)
    def _():
        data0[WINDOW, 0, xm, y] = jnp.zeros((16, 128), jnp.bfloat16)

    edges = len(near) + jnp.where(t > 0, 1, 0) + jnp.where(t < NT - 1, 1, 0)
    pl.semaphore_wait(barrier, edges)

    def spread_b(o):
        for d in ONWARD.get(o, ()):
            send(part_b(xm, o, y), ("bz", o ^ d), along[d], part_b(xm, o ^ d, y))
        send(part_b(xm, o, y), ("b_dn", o), up)
        send(part_b(xm, o, y), ("b_up", o), dn)
        send(part_b(xm, o, y), ("b_mate", o, 0), mate)

    def spread_a(o):
        for d in ONWARD.get(o, ()):
            send(part_a(o, y), ("az", o ^ d), along[d], part_a(o ^ d, y))
        send(part_a(o, y), ("a_dn", o), up)
        send(part_a(o, y), ("a_up", o), dn)

    send(half_a(xm, 0, y), ("a_mate",), mate)
    spread_b(0)
    send(own(WINDOW - 1), ("right",), (h, t + 1), own(WINDOW + 1), t < NT - 1)
    send(own(0), ("left",), (h, t - 1), own(WINDOW), t > 0)
    send(cos_ref, ("cos",), partner, cos_far)
    send(sin_ref, ("sin",), partner, sin_far)
    send(blk_v, ("blocks",), partner, blk_far)
    for s in range(4):
        send(w_ref.at[s], ("weights", s), partner, w_far.at[s])

    def rotation(slab, cosine, sine):
        wide_shape = (NH, HALF * 16)
        column = lax.broadcasted_iota(jnp.int32, wide_shape, 1)
        row = lax.broadcasted_iota(jnp.int32, wide_shape, 0)
        z_of = lax.shift_right_logical(column, 7)
        z_of = jnp.bitwise_xor(z_of, jnp.full(wide_shape, z, jnp.int32))
        x_of = jnp.bitwise_and(lax.shift_right_logical(column, 6), 1) + 2 * half
        y_of = jnp.bitwise_and(lax.shift_right_logical(column, 4), 3)
        expand = ((x_of * NZ + z_of) * NY + y_of == row).astype(jnp.float32).astype(jnp.bfloat16)
        same = jnp.bitwise_and(column, 15) == jnp.bitwise_and(row, 15)
        rows = []
        for layer in range(4):
            rows += [cosine[layer], -sine[layer]]
        for layer in range(4):
            rows += [sine[layer], cosine[layer]]
        table = jnp.concatenate(rows, axis=0)
        high = table.astype(jnp.bfloat16)
        low = (table - high.astype(jnp.float32)).astype(jnp.bfloat16)
        halves = []
        for piece in (high, low):
            wide = jnp.dot(piece, expand, preferred_element_type=jnp.float32)
            wide = jnp.where(same, wide, 0.0)
            halves.append(jnp.sum(wide.reshape(8, 16, HALF * 16), axis=1))
        rot[slab] = jnp.concatenate(halves, axis=0).astype(jnp.bfloat16)

    rotation(0, cos_ref, sin_ref)
    for copy in copies[len(first_copies) :]:
        copy.wait()

    for o in range(NZ):

        @pl.loop(0, 2 * NY)
        def _(n):
            m, yi = lax.div(n, NY), lax.rem(n, NY)
            sector = sector_ref[((2 * half + m) * NZ + z_at(o)) * NY + yi]
            for s in range(4):
                one = jnp.where(sector == s, 1.0, 0.0).astype(jnp.float32)
                mask[s, o, m, yi] = jnp.full((16, 128), one, jnp.float32).astype(jnp.bfloat16)

    for slab in range(2):
        vol[slab] = jnp.zeros((8, 512), jnp.float32)

    def focus(g, slab):
        weights, blocks = ((w_own, blk_ref), (w_far, blk_smem))[slab]
        rotate = rot[slab, :, g * 256 : (g + 1) * 256]
        chosen = [mask[s, 2 * g : 2 * g + 2].reshape(16, 16, 128) for s in range(4)]
        for u in range(4):
            lanes = slice(u * 128, (u + 1) * 128)
            pieces = []
            for s in range(4):
                for k in range(3):
                    picked = data[g][lax.rem(blocks[k, s, u] + (BLOCKS - 1), BLOCKS)]
                    pieces.append((picked.reshape(16, 16, 128) * chosen[s]).reshape(256, 128))
            amplitude = jnp.dot(
                jnp.concatenate(pieces, axis=1), weights[:, u].reshape(12 * 128, 128),
                preferred_element_type=jnp.float32,
            ).reshape(16, 2, 8, 128)
            re, im = amplitude[:, 0], amplitude[:, 1]
            pc = gcos[2 * g : 2 * g + 2, :, :, :, lanes].reshape(16, 8, 128).astype(jnp.float32)
            ps = gsin[2 * g : 2 * g + 2, :, :, :, lanes].reshape(16, 8, 128).astype(jnp.float32)
            turned = jnp.concatenate([re * pc - im * ps, re * ps + im * pc], axis=1).reshape(256, 128)
            high = turned.astype(jnp.bfloat16)
            low = (turned - high.astype(jnp.float32)).astype(jnp.bfloat16)
            layers = jnp.dot(rotate, high, preferred_element_type=jnp.float32)
            layers = layers + jnp.dot(rotate, low, preferred_element_type=jnp.float32)
            vol[slab, :, lanes] += layers[:8] + layers[8:]

    complete, far_ready, told = set(), [], []

    def finish(g):
        if g in complete:
            return
        complete.add(g)
        for o in (2 * g, 2 * g + 1):
            for n, yi in enumerate((y, y_dn, y_up, y_far)):
                got(part_b(1 - xm, o, yi), ("b_mate", o, n))
            for m in range(2):
                got(half_a(m, o, y_far), ("a_far", m, o))
        for n, yi in enumerate((y_dn, y_up, y_far)):
            got(ends_all(g, yi), ("ends", n, g))

    def weights_from_afar():
        if far_ready:
            return
        got(cos_far, ("cos",))
        got(sin_far, ("sin",))
        got(blk_far, ("blocks",))
        copy = pltpu.make_async_copy(blk_far, blk_smem, lsem.at[N_LOCAL - 1])
        copy.start()
        rotation(1, cos_far, sin_far)
        copy.wait()
        for s in range(4):
            got(w_far.at[s], ("weights", s))
        far_ready.append(True)

    def give(slab, slot, device, condition=None):
        send(vol.at[slab], ("volume", slot), device, vol_in.at[slot], condition)

    for what, o, *more in ORDER:
        if what == A_MATE:
            got(half_a(1 - xm, 0, y), ("a_mate",))
            spread_a(0)
        elif what == B_Z:
            got(part_b(xm, o, y), ("bz", o))
            spread_b(o)
        elif what == A_Z:
            got(part_a(o, y), ("az", o))
            spread_a(o)
        elif what == B_DN:
            got(part_b(xm, o, y_dn), ("b_dn", o))
            send(half_b(0, o, y_dn), ("b_far", 0, o), up)
            send(part_b(xm, o, y_dn), ("b_mate", o, 1), mate)
        elif what == B_UP:
            got(part_b(xm, o, y_up), ("b_up", o))
            send(half_b(1, o, y_up), ("b_far", 1, o), dn)
            send(part_b(xm, o, y_up), ("b_mate", o, 2), mate)
        elif what == B_FAR:
            for n in range(2):
                got(half_b(n, o, y_far), ("b_far", n, o))
            send(part_b(xm, o, y_far), ("b_mate", o, 3), mate)
        elif what == A_DN:
            got(part_a(o, y_dn), ("a_dn", o))
            send(half_a(0, o, y_dn), ("a_far", 0, o), up)
        elif what == A_UP:
            got(part_a(o, y_up), ("a_up", o))
            send(half_a(1, o, y_up), ("a_far", 1, o), dn)
        elif what == ENDS:
            pl.when(t > 0)(lambda: got(own(WINDOW + 1), ("right",)))
            pl.when(t < NT - 1)(lambda: got(own(WINDOW), ("left",)))
            mine = data0.at[pl.ds(WINDOW, 2), 0, xm, y]
            send(mine, ("ends_mate",), mate)
        elif what == ENDS_MATE:
            got(data0.at[pl.ds(WINDOW, 2), 0, 1 - xm, y], ("ends_mate",))
            for d in range(NZ - 1, 0, -1):
                send(ends(0, y), ("ends_z", d), along[d], ends(d, y))
        elif what == ENDS_Z:
            for d in range(1, NZ):
                got(ends(d, y), ("ends_z", d))
            for g in range(GROUPS):
                for n, device in enumerate((up, dn, opposite)):
                    send(ends_all(g, y), ("ends", n, g), device)
        elif what == FOCUS:
            finish(o)
            if more[0] == 1:
                weights_from_afar()
            if len(complete) == GROUPS and not told:
                pl.semaphore_signal(ready, inc=1, device_id=partner, device_id_type=MESH)
                told.append(True)
            focus(o, more[0])
            retire()
            if (o, more[0]) == (GROUPS - 1, 1):
                give(1, 0, partner)
                pl.semaphore_wait(ready, 1)
                give(1, 3, (hp + 1, t), hp < NH - 1)
                give(1, 4, (hp - 1, t), hp > 0)
    give(0, 1, (h + 1, t), h < NH - 1)
    give(0, 2, (h - 1, t), h > 0)

    def take(slot):
        got(vol_in.at[slot], ("volume", slot))

    @pl.when(h > 0)
    def _():
        take(3)
        take(1)

    @pl.when(h == 0)
    def _():
        vol_in[1] = jnp.zeros((8, 512), jnp.float32)
        vol_in[3] = jnp.zeros((8, 512), jnp.float32)

    @pl.when(h < NH - 1)
    def _():
        take(4)
        take(2)

    @pl.when(h == NH - 1)
    def _():
        vol_in[2] = jnp.zeros((8, 512), jnp.float32)
        vol_in[4] = jnp.zeros((8, 512), jnp.float32)

    take(0)
    here = vol[0] + vol_in[0]
    below = vol_in[1] + vol_in[3]
    above = vol_in[2] + vol_in[4]
    for part in range(2):
        rows = jnp.concatenate(
            [below[4 * part + 2 : 4 * part + 4], here[4 * part : 4 * part + 4], above[4 * part : 4 * part + 2]], axis=0
        )
        image = jnp.zeros((4, 512), jnp.float32)
        for j in range(5):
            image = image + taps_ref[j] * rows[j : j + 4]
        out_ref[part] = image * (1.0 / math.sqrt(8 * NH))

    retire()
    retire()


def local(pulse_panels, interp_weights, range_blocks, sector_of_panel, layer_cos, layer_sin, ground_cos, ground_sin, height_kernel):
    blocks = jnp.transpose(range_blocks[0], (2, 0, 1))
    f32, bf16, i32 = jnp.float32, jnp.bfloat16, jnp.int32
    ground = (2, 2, NZ, NY, 8, 512)
    return pl.pallas_call(
        kernel,
        out_shape=jax.ShapeDtypeStruct((2, 4, 512), f32),
        in_specs=[pl.BlockSpec(memory_space=pl.ANY)] * 9,
        out_specs=pl.BlockSpec(memory_space=pltpu.VMEM),
        scratch_shapes=[
            pltpu.VMEM((2, 8, WINDOW * 128), bf16),
            pltpu.VMEM((3, 4, 4), i32),
            pltpu.SMEM((3, 4, 4), i32),
            pltpu.SMEM((NH,), i32),
            pltpu.VMEM((4, 8, NH), f32),
            pltpu.VMEM((4, 8, NH), f32),
            pltpu.SMEM((5,), f32),
        ]
        + [pltpu.VMEM((BLOCKS, 2, 2, NY, 16, 128), bf16)] * GROUPS
        + [
            pltpu.VMEM((4, 4, 3, 128, 128), bf16),
            pltpu.VMEM((4, 4, 3, 128, 128), bf16),
            pltpu.VMEM((3, 4, 4), i32),
            pltpu.SMEM((3, 4, 4), i32),
            pltpu.VMEM((4, 8, NH), f32),
            pltpu.VMEM((4, 8, NH), f32),
            pltpu.VMEM((NZ, 2, NY, 8, 512), bf16),
            pltpu.VMEM((NZ, 2, NY, 8, 512), bf16),
            pltpu.VMEM((4, NZ, 2, NY, 16, 128), bf16),
            pltpu.VMEM((2, 16, HALF * 16), bf16),
            pltpu.VMEM((2, 8, 512), f32),
            pltpu.VMEM((5, 8, 512), f32),
            pltpu.SemaphoreType.DMA((N_SEND,)),
            pltpu.SemaphoreType.DMA((N_RECEIVE,)),
            pltpu.SemaphoreType.DMA((N_LOCAL + 1,)),
            pltpu.SemaphoreType.REGULAR,
        ],
        compiler_params=pltpu.CompilerParams(collective_id=0, has_side_effects=True, vmem_limit_bytes=62 << 20),
        name="focus",
    )(
        pulse_panels[0], interp_weights[0], blocks, sector_of_panel,
        jnp.swapaxes(layer_cos, 1, 2), jnp.swapaxes(layer_sin, 1, 2),
        ground_cos.reshape(ground), ground_sin.reshape(ground), height_kernel,
    )


def solution(mesh):
    in_specs = (
        P("height", None, None, "tile"),
        P("height", None, "tile", None, None, None),
        P("height", None, "tile", None),
        P(),
        P("height", None, None),
        P("height", None, None),
        P(None, None, "tile"),
        P(None, None, "tile"),
        P(),
    )
    return jax.shard_map(local, mesh=mesh, in_specs=in_specs, out_specs=P(None, "height", "tile"), check_vma=False)
```

time: 1200 us -> 81 us (0.07)
  the two profiles are of different devices: /device:TPU:8 before, /device:TPU:6 now
where the time goes in v2:
time: 81 us; the launch traced here: 79.8 us
  Pallas kernels  78.4 us (97%)
  local copies, waits for them, and re-layouts  1.32 us (2%)
    pallas_call x1, Pallas kernels, local(): pl.pallas_call(kernel, out_shape=jax.ShapeDtypeStruct((2, 4, 512), f32),...  78.4 us

profile of v2, /device:TPU:6, one launch (start us, length us, event | category | flops | bytes accessed | tf_op | source)
XLA Modules:
  0.0 79.8 jit_solution(11733757518826079116)
XLA Ops:
  0.0 78.4 %focus.1 = f32[2,4,512]{2,1,0:T(4,128)} custom-call(bf16[2,8,3072]{2,1,0:T(8,128)(2,1)} %bitcast.12, bf16[4,4,3,128,128]{4,3,2,1,0:T(8,128)(2,1)} %bitcast.9, s32[3,4,4]{2,1,0:T(4,128)} %bitcast.15, s32[128]{0:T(128)} %sector_hbm.1, f32[4,8,128]{2,1,0:T(8,128)} %bitcast.13, f32[4,8,128]{2,1,0:T(8,128)} %bitcast.14, bf16[2,2,8,4,8,512]{5,4,3,2,1,0:T(8,128)(2,1)} %bitcast.10, ...), custom_call_target="tpu_custom_call" | custom-call | tf_op jit(solution)/shard_map/focus/pallas_call | solution.py:389
  78.4 1.3 %copy.11 = f32[2,4,512]{2,1,0:T(4,128)} copy(f32[2,4,512]{2,1,0:T(4,128)} %focus.1) | data formatting | bytes 32768

commit v3 on v2

--- a/solution.py
+++ b/solution.py
@@ -17,15 +17,16 @@
 PART = 10
 GROUPS = NZ // 2
 
-A_MATE, B_Z, A_Z, B_DN, B_UP, B_FAR, A_DN, A_UP, ENDS, ENDS_MATE, ENDS_Z, FOCUS = range(12)
+A_MATE, B_Z, A_Z, B_DN, B_UP, B_FAR, A_DN, A_UP, ENDS, ENDS_MATE, ENDS_Z, COMPLETE, FOCUS = range(13)
 ORDER = (
-    (A_MATE, 0), (B_Z, 1), (B_DN, 0), (B_UP, 0), (B_Z, 2), (ENDS, 0), (A_Z, 1), (A_DN, 0), (A_UP, 0), (B_DN, 1),
-    (B_UP, 1), (B_Z, 4), (B_Z, 3), (B_FAR, 0), (A_Z, 2), (B_DN, 2), (B_UP, 2), (A_DN, 1), (A_UP, 1), (B_Z, 5),
-    (B_FAR, 1), (A_Z, 3), (B_Z, 6), (B_DN, 4), (B_UP, 4), (A_Z, 4), (B_DN, 3), (B_UP, 3), (A_DN, 2), (A_UP, 2),
-    (B_FAR, 2), (B_Z, 7), (ENDS_MATE, 0), (A_Z, 5), (B_DN, 5), (B_UP, 5), (A_DN, 3), (A_UP, 3), (A_Z, 6), (B_DN, 6),
-    (ENDS_Z, 0), (B_UP, 6), (B_FAR, 4), (A_DN, 4), (A_UP, 4), (B_FAR, 3), (A_Z, 7), (B_DN, 7), (B_UP, 7),
-    (FOCUS, 0, 0), (A_DN, 5), (A_UP, 5), (B_FAR, 5), (FOCUS, 0, 1), (A_DN, 6), (A_UP, 6), (B_FAR, 6), (FOCUS, 1, 0),
-    (FOCUS, 1, 1), (A_DN, 7), (A_UP, 7), (B_FAR, 7), (FOCUS, 2, 0), (FOCUS, 2, 1), (FOCUS, 3, 1), (FOCUS, 3, 0),
+    (A_MATE, 0), (B_DN, 0), (B_UP, 0), (B_Z, 1), (ENDS, 0), (B_Z, 2), (A_DN, 0), (A_UP, 0), (B_FAR, 0), (B_Z, 4),
+    (A_Z, 1), (B_DN, 1), (B_UP, 1), (B_DN, 2), (B_UP, 2), (A_Z, 2), (B_Z, 3), (B_DN, 4), (B_UP, 4), (B_Z, 5),
+    (A_DN, 1), (A_UP, 1), (B_FAR, 1), (A_Z, 4), (B_Z, 6), (B_FAR, 2), (A_DN, 2), (A_UP, 2), (A_Z, 3), (B_DN, 3),
+    (B_UP, 3), (B_FAR, 4), (B_DN, 5), (B_UP, 5), (A_Z, 5), (A_DN, 4), (A_UP, 4), (A_Z, 6), (B_Z, 7), (ENDS_MATE, 0),
+    (B_DN, 6), (B_UP, 6), (A_DN, 3), (A_UP, 3), (B_FAR, 3), (B_FAR, 5), (A_DN, 5), (A_UP, 5), (A_Z, 7), (ENDS_Z, 0),
+    (A_DN, 6), (A_UP, 6), (B_DN, 7), (B_UP, 7), (B_FAR, 6), (A_DN, 7), (A_UP, 7), (COMPLETE, 0), (COMPLETE, 1),
+    (COMPLETE, 2), (B_FAR, 7), (FOCUS, 0, 0), (FOCUS, 0, 1), (FOCUS, 1, 0), (FOCUS, 1, 1), (COMPLETE, 3),
+    (FOCUS, 2, 0), (FOCUS, 2, 1), (FOCUS, 3, 1), (FOCUS, 3, 0),
 )
 ONWARD = {0: (4, 2, 1), 4: (2, 1), 2: (1,), 6: (1,)}
 N_SEND, N_RECEIVE, N_LOCAL = 256, 224, 24
@@ -87,7 +88,7 @@
     def retire():
         for number in range(*retired):
             source, condition = sends[number]
-            copy = edge(source, source, number, ("a_mate",), mate)
+            copy = edge(source, source, number, ("a_mate", 0), mate)
             if condition is None:
                 copy.wait_send()
             else:
@@ -104,14 +105,19 @@
         return data[o // 2].at[pl.ds(PART, WINDOW - PART), o % 2, m, yi]
 
     def half_b(n, o, yi):
-        size = (WINDOW - PART) // 2
-        return data[o // 2].at[pl.ds(PART + n * size, size), o % 2, xm, yi]
+        middle = (WINDOW + PART) // 2
+        start, stop = ((PART, middle), (middle, WINDOW))[n]
+        return data[o // 2].at[pl.ds(start, stop - start), o % 2, xm, yi]
+
+    core = lax.rem(t, 2)
+    inner = lax.rem(t + 1, NT) >= 2
+    far_block = WINDOW + lax.div(t, 2)
 
     def ends(o, yi):
-        return data[o // 2].at[pl.ds(WINDOW, 2), o % 2, :, yi]
+        return data[o // 2].at[far_block, o % 2, :, yi]
 
     def ends_all(g, yi):
-        return data[g].at[pl.ds(WINDOW, 2), :, :, yi]
+        return data[g].at[far_block, :, :, yi]
 
     def own(block):
         return data0.at[block, 0, xm, y]
@@ -129,7 +135,7 @@
     def _():
         greet((h, t + 1))
 
-    near = [along[4], along[2], along[1], opposite, up, dn, mate, partner]
+    near = [along[4], along[3], along[2], along[1], opposite, up, dn, mate, partner]
     for device in near:
         greet(device)
 
@@ -150,13 +156,10 @@
         lanes = slice(b * 128, (b + 1) * 128)
         data0[b, 0, xm, y] = jnp.concatenate([x_ref[0, :, lanes], x_ref[1, :, lanes]], axis=0)
 
-    @pl.when(t == 0)
-    def _():
-        data0[WINDOW + 1, 0, xm, y] = jnp.zeros((16, 128), jnp.bfloat16)
-
-    @pl.when(t == NT - 1)
-    def _():
-        data0[WINDOW, 0, xm, y] = jnp.zeros((16, 128), jnp.bfloat16)
+    @pl.when(jnp.logical_not(inner))
+    def _():
+        for ref in data:
+            ref[WINDOW + 1 - lax.div(t, 2)] = jnp.zeros((2, 2, NY, 16, 128), jnp.bfloat16)
 
     edges = len(near) + jnp.where(t > 0, 1, 0) + jnp.where(t < NT - 1, 1, 0)
     pl.semaphore_wait(barrier, edges)
@@ -174,10 +177,10 @@
         send(part_a(o, y), ("a_dn", o), up)
         send(part_a(o, y), ("a_up", o), dn)
 
-    send(half_a(xm, 0, y), ("a_mate",), mate)
+    send(half_a(xm, 0, y), ("a_mate", 0), mate)
     spread_b(0)
-    send(own(WINDOW - 1), ("right",), (h, t + 1), own(WINDOW + 1), t < NT - 1)
-    send(own(0), ("left",), (h, t - 1), own(WINDOW), t > 0)
+    send(own(WINDOW - 1), ("right",), (h, t + 1), own(WINDOW + 1), t == 1)
+    send(own(0), ("left",), (h, t - 1), own(WINDOW), t == 2)
     send(cos_ref, ("cos",), partner, cos_far)
     send(sin_ref, ("sin",), partner, sin_far)
     send(blk_v, ("blocks",), partner, blk_far)
@@ -254,16 +257,18 @@
     complete, far_ready, told = set(), [], []
 
     def finish(g):
-        if g in complete:
-            return
-        complete.add(g)
         for o in (2 * g, 2 * g + 1):
             for n, yi in enumerate((y, y_dn, y_up, y_far)):
                 got(part_b(1 - xm, o, yi), ("b_mate", o, n))
             for m in range(2):
                 got(half_a(m, o, y_far), ("a_far", m, o))
-        for n, yi in enumerate((y_dn, y_up, y_far)):
-            got(ends_all(g, yi), ("ends", n, g))
+
+        @pl.when(inner)
+        def _():
+            for n, yi in enumerate((y_dn, y_up, y_far)):
+                got(ends_all(g, yi), ("ends", n, g))
+
+        send(data[g].at[(WINDOW - 1) * (1 - core)], ("core", g), (h, t + 1 - 2 * core), data[g].at[WINDOW + 1 - core])
 
     def weights_from_afar():
         if far_ready:
@@ -284,7 +289,7 @@
 
     for what, o, *more in ORDER:
         if what == A_MATE:
-            got(half_a(1 - xm, 0, y), ("a_mate",))
+            got(half_a(1 - xm, 0, y), ("a_mate", 0))
             spread_a(0)
         elif what == B_Z:
             got(part_b(xm, o, y), ("bz", o))
@@ -311,22 +316,29 @@
             got(part_a(o, y_up), ("a_up", o))
             send(half_a(1, o, y_up), ("a_far", 1, o), dn)
         elif what == ENDS:
-            pl.when(t > 0)(lambda: got(own(WINDOW + 1), ("right",)))
-            pl.when(t < NT - 1)(lambda: got(own(WINDOW), ("left",)))
-            mine = data0.at[pl.ds(WINDOW, 2), 0, xm, y]
-            send(mine, ("ends_mate",), mate)
+            pl.when(t == 2)(lambda: got(own(WINDOW + 1), ("right",)))
+            pl.when(t == 1)(lambda: got(own(WINDOW), ("left",)))
+            send(data0.at[far_block, 0, xm, y], ("ends_mate",), mate, condition=inner)
         elif what == ENDS_MATE:
-            got(data0.at[pl.ds(WINDOW, 2), 0, 1 - xm, y], ("ends_mate",))
+            pl.when(inner)(lambda: got(data0.at[far_block, 0, 1 - xm, y], ("ends_mate",)))
             for d in range(NZ - 1, 0, -1):
-                send(ends(0, y), ("ends_z", d), along[d], ends(d, y))
+                send(ends(0, y), ("ends_z", d), along[d], ends(d, y), inner)
         elif what == ENDS_Z:
-            for d in range(1, NZ):
-                got(ends(d, y), ("ends_z", d))
+
+            @pl.when(inner)
+            def _():
+                for d in range(1, NZ):
+                    got(ends(d, y), ("ends_z", d))
+
             for g in range(GROUPS):
                 for n, device in enumerate((up, dn, opposite)):
-                    send(ends_all(g, y), ("ends", n, g), device)
+                    send(ends_all(g, y), ("ends", n, g), device, condition=inner)
+        elif what == COMPLETE:
+            finish(o)
         elif what == FOCUS:
-            finish(o)
+            if o not in complete:
+                complete.add(o)
+                got(data[o].at[WINDOW + core], ("core", o))
             if more[0] == 1:
                 weights_from_afar()
             if len(complete) == GROUPS and not told:

time: 81 us -> 82.1 us (1.014)
  Pallas kernels: 78.4 us -> 79.3 us
    pallas_call x1, Pallas kernels: 78.4 us -> 79.3 us  [local(): pl.pallas_call(kernel, out_shape=jax.ShapeDtypeStruct((2, 4, 512), f32),...]
where the time goes in v3:
time: 82.1 us; the launch traced here: 80.6 us
  Pallas kernels  79.3 us (97%)
  local copies, waits for them, and re-layouts  1.32 us (2%)
    pallas_call x1, Pallas kernels, local(): pl.pallas_call(kernel, out_shape=jax.ShapeDtypeStruct((2, 4, 512), f32),...  79.3 us

profile of v3, /device:TPU:6, one launch (start us, length us, event | category | flops | bytes accessed | tf_op | source)
XLA Modules:
  0.0 80.6 jit_solution(6953055635116236900)
XLA Ops:
  0.0 79.3 %focus.1 = f32[2,4,512]{2,1,0:T(4,128)} custom-call(bf16[2,8,3072]{2,1,0:T(8,128)(2,1)} %bitcast.12, bf16[4,4,3,128,128]{4,3,2,1,0:T(8,128)(2,1)} %bitcast.9, s32[3,4,4]{2,1,0:T(4,128)} %bitcast.15, s32[128]{0:T(128)} %sector_hbm.1, f32[4,8,128]{2,1,0:T(8,128)} %bitcast.13, f32[4,8,128]{2,1,0:T(8,128)} %bitcast.14, bf16[2,2,8,4,8,512]{5,4,3,2,1,0:T(8,128)(2,1)} %bitcast.10, ...), custom_call_target="tpu_custom_call" | custom-call | tf_op jit(solution)/shard_map/focus/pallas_call | solution.py:401
  79.3 1.3 %copy.11 = f32[2,4,512]{2,1,0:T(4,128)} copy(f32[2,4,512]{2,1,0:T(4,128)} %focus.1) | data formatting | bytes 32768

commit v4 on v3

--- a/solution.py
+++ b/solution.py
@@ -17,25 +17,27 @@
 PART = 10
 GROUPS = NZ // 2
 
-A_MATE, B_Z, A_Z, B_DN, B_UP, B_FAR, A_DN, A_UP, ENDS, ENDS_MATE, ENDS_Z, COMPLETE, FOCUS = range(13)
+A_MATE, B_Z, A_Z, B_DN, B_UP, B_FAR, A_DN, A_UP, ENDS, ENDS_MATE, ENDS_Z, ENDS_Y, COMPLETE, FOCUS = range(14)
 ORDER = (
-    (A_MATE, 0), (B_DN, 0), (B_UP, 0), (B_Z, 1), (ENDS, 0), (B_Z, 2), (A_DN, 0), (A_UP, 0), (B_FAR, 0), (B_Z, 4),
-    (A_Z, 1), (B_DN, 1), (B_UP, 1), (B_DN, 2), (B_UP, 2), (A_Z, 2), (B_Z, 3), (B_DN, 4), (B_UP, 4), (B_Z, 5),
-    (A_DN, 1), (A_UP, 1), (B_FAR, 1), (A_Z, 4), (B_Z, 6), (B_FAR, 2), (A_DN, 2), (A_UP, 2), (A_Z, 3), (B_DN, 3),
-    (B_UP, 3), (B_FAR, 4), (B_DN, 5), (B_UP, 5), (A_Z, 5), (A_DN, 4), (A_UP, 4), (A_Z, 6), (B_Z, 7), (ENDS_MATE, 0),
-    (B_DN, 6), (B_UP, 6), (A_DN, 3), (A_UP, 3), (B_FAR, 3), (B_FAR, 5), (A_DN, 5), (A_UP, 5), (A_Z, 7), (ENDS_Z, 0),
-    (A_DN, 6), (A_UP, 6), (B_DN, 7), (B_UP, 7), (B_FAR, 6), (A_DN, 7), (A_UP, 7), (COMPLETE, 0), (COMPLETE, 1),
-    (COMPLETE, 2), (B_FAR, 7), (FOCUS, 0, 0), (FOCUS, 0, 1), (FOCUS, 1, 0), (FOCUS, 1, 1), (COMPLETE, 3),
-    (FOCUS, 2, 0), (FOCUS, 2, 1), (FOCUS, 3, 1), (FOCUS, 3, 0),
+    (A_MATE, 0), (B_DN, 0), (B_UP, 0), (B_Z, 1), (B_Z, 2), (ENDS, 0), (A_DN, 0), (A_UP, 0), (B_FAR, 0), (A_Z, 1),
+    (B_Z, 4), (B_DN, 1), (B_UP, 1), (B_DN, 2), (B_UP, 2), (A_Z, 2), (B_Z, 3), (ENDS_MATE, 0), (A_DN, 1), (A_UP, 1),
+    (B_Z, 5), (ENDS_Z, 1), (B_DN, 4), (B_UP, 4), (ENDS_Z, 2), (B_FAR, 1), (B_Z, 6), (B_FAR, 2), (A_Z, 4),
+    (ENDS_Z, 4), (A_Z, 3), (A_DN, 2), (A_UP, 2), (ENDS_Z, 3), (B_DN, 3), (B_UP, 3), (ENDS_Z, 5), (ENDS_Z, 6),
+    (B_Z, 7), (B_DN, 5), (B_UP, 5), (B_FAR, 4), (B_DN, 6), (B_UP, 6), (ENDS_Z, 7), (ENDS_Y, 0), (A_Z, 5), (A_Z, 6),
+    (A_DN, 4), (A_UP, 4), (A_DN, 3), (A_UP, 3), (B_FAR, 3), (B_DN, 7), (B_UP, 7), (A_Z, 7), (B_FAR, 5), (B_FAR, 6),
+    (COMPLETE, 0), (A_DN, 5), (A_UP, 5), (FOCUS, 0, 0), (A_DN, 6), (A_UP, 6), (FOCUS, 0, 1), (B_FAR, 7),
+    (COMPLETE, 1), (A_DN, 7), (A_UP, 7), (FOCUS, 1, 0), (FOCUS, 1, 1), (COMPLETE, 2), (FOCUS, 2, 0), (COMPLETE, 3),
+    (FOCUS, 2, 1), (FOCUS, 3, 1), (FOCUS, 3, 0),
 )
 ONWARD = {0: (4, 2, 1), 4: (2, 1), 2: (1,), 6: (1,)}
+IN_FLIGHT = 6
 N_SEND, N_RECEIVE, N_LOCAL = 256, 224, 24
 
 
 def kernel(
     x_hbm, w_ref, blk_hbm, sector_hbm, cos_hbm, sin_hbm, gc_ref, gs_ref, taps_hbm, out_ref,
     x_ref, blk_v, blk_ref, sector_ref, cos_ref, sin_ref, taps_ref, data0, data1, data2, data3,
-    w_own, w_far, blk_far, blk_smem, cos_far, sin_far, gcos, gsin, mask, rot, vol, vol_in,
+    w_own, w_far, blk_far, blk_smem, cos_far, sin_far, gcos, gsin, sectors, rot, vol, vol_in,
     ssem, rsem, lsem, ready,
 ):
     data = (data0, data1, data2, data3)
@@ -53,6 +55,9 @@
                 flipped = flipped + bit - 2 * bit * lax.rem(lax.div(z, bit), 2)
         return flipped
 
+    def panel_at(o, m, yi):
+        return ((2 * half + m) * NZ + z_at(o)) * NY + yi
+
     y_up, y_dn, y_far = lax.rem(y + 1, NY), lax.rem(y + 3, NY), lax.rem(y + 2, NY)
     mate = place(x + 1 - 2 * xm, z, y)
     partner = place(3 - x, z, y)
@@ -60,7 +65,18 @@
     along = [place(x, z_at(d), y) for d in range(NZ)]
     hp = partner[0]
 
-    receive_ids, sends = {}, []
+    middle, edge_next, beside_edge = (
+        jnp.logical_or(z == a, z == NZ - 1 - a) for a in (3, 2, 1)
+    )
+    inside = jnp.logical_or(edge_next, beside_edge)
+
+    def onward(o):
+        ways = [(d, beside_edge if (o, d) in ((2, 1), (6, 1)) else None) for d in ONWARD.get(o, ())]
+        if o in (0, 4):
+            ways += [(3, inside), (7, middle)]
+        return ways
+
+    receive_ids, sends, waited = {}, [], set()
 
     def receive_id(key):
         return receive_ids.setdefault(key, len(receive_ids))
@@ -80,6 +96,17 @@
         else:
             pl.when(condition)(copy.start)
 
+    to_mate = []
+
+    def send_mate(source, key):
+        to_mate.append(len(sends))
+        if len(to_mate) > IN_FLIGHT:
+            number = to_mate[-1 - IN_FLIGHT]
+            if number not in waited:
+                edge(sends[number][0], sends[number][0], number, key, mate).wait_send()
+                waited.add(number)
+        send(source, key, mate)
+
     def got(region, key):
         edge(region, region, 0, key, mate).wait_recv()
 
@@ -88,6 +115,9 @@
     def retire():
         for number in range(*retired):
             source, condition = sends[number]
+            if number in waited:
+                continue
+            waited.add(number)
             copy = edge(source, source, number, ("a_mate", 0), mate)
             if condition is None:
                 copy.wait_send()
@@ -135,9 +165,18 @@
     def _():
         greet((h, t + 1))
 
-    near = [along[4], along[3], along[2], along[1], opposite, up, dn, mate, partner]
+    near = [along[4], along[2], along[1], opposite, up, dn, mate, partner]
     for device in near:
         greet(device)
+
+    @pl.when(inside)
+    def _():
+        greet(along[3])
+
+    @pl.when(middle)
+    def _():
+        greet(along[7])
+
 
     local_copies = [
         (w_ref, w_own), (sector_hbm, sector_ref), (taps_hbm, taps_ref), (blk_hbm, blk_ref),
@@ -162,20 +201,26 @@
             ref[WINDOW + 1 - lax.div(t, 2)] = jnp.zeros((2, 2, NY, 16, 128), jnp.bfloat16)
 
     edges = len(near) + jnp.where(t > 0, 1, 0) + jnp.where(t < NT - 1, 1, 0)
+    edges = edges + jnp.where(jnp.logical_or(inside, middle), 1, 0)
     pl.semaphore_wait(barrier, edges)
 
     def spread_b(o):
-        for d in ONWARD.get(o, ()):
-            send(part_b(xm, o, y), ("bz", o ^ d), along[d], part_b(xm, o ^ d, y))
+        for d, condition in onward(o):
+            send(part_b(xm, o, y), ("bz", o ^ d), along[d], part_b(xm, o ^ d, y), condition)
         send(part_b(xm, o, y), ("b_dn", o), up)
         send(part_b(xm, o, y), ("b_up", o), dn)
-        send(part_b(xm, o, y), ("b_mate", o, 0), mate)
+        send_mate(part_b(xm, o, y), ("b_mate", o, 0))
 
     def spread_a(o):
-        for d in ONWARD.get(o, ()):
-            send(part_a(o, y), ("az", o ^ d), along[d], part_a(o ^ d, y))
+        for d, condition in onward(o):
+            send(part_a(o, y), ("az", o ^ d), along[d], part_a(o ^ d, y), condition)
         send(part_a(o, y), ("a_dn", o), up)
         send(part_a(o, y), ("a_up", o), dn)
+
+    def spread_ends(o):
+        for d, condition in onward(o):
+            both = inner if condition is None else jnp.logical_and(inner, condition)
+            send(ends(o, y), ("ends_z", o ^ d), along[d], ends(o ^ d, y), both)
 
     send(half_a(xm, 0, y), ("a_mate", 0), mate)
     spread_b(0)
@@ -221,10 +266,7 @@
         @pl.loop(0, 2 * NY)
         def _(n):
             m, yi = lax.div(n, NY), lax.rem(n, NY)
-            sector = sector_ref[((2 * half + m) * NZ + z_at(o)) * NY + yi]
-            for s in range(4):
-                one = jnp.where(sector == s, 1.0, 0.0).astype(jnp.float32)
-                mask[s, o, m, yi] = jnp.full((16, 128), one, jnp.float32).astype(jnp.bfloat16)
+            sectors[o, m, yi] = jnp.full((16, 128), sector_ref[panel_at(o, m, yi)], jnp.int32)
 
     for slab in range(2):
         vol[slab] = jnp.zeros((8, 512), jnp.float32)
@@ -232,27 +274,37 @@
     def focus(g, slab):
         weights, blocks = ((w_own, blk_ref), (w_far, blk_smem))[slab]
         rotate = rot[slab, :, g * 256 : (g + 1) * 256]
-        chosen = [mask[s, 2 * g : 2 * g + 2].reshape(16, 16, 128) for s in range(4)]
+        of_rows = sectors[2 * g : 2 * g + 2].reshape(256, 128)
+        places = [(n, m, yi) for n in range(2) for m in range(2) for yi in range(NY)]
+        chosen = [sector_ref[panel_at(2 * g + n, m, yi)] for n, m, yi in places]
+        highs, lows = [], []
         for u in range(4):
             lanes = slice(u * 128, (u + 1) * 128)
-            pieces = []
-            for s in range(4):
-                for k in range(3):
-                    picked = data[g][lax.rem(blocks[k, s, u] + (BLOCKS - 1), BLOCKS)]
-                    pieces.append((picked.reshape(16, 16, 128) * chosen[s]).reshape(256, 128))
-            amplitude = jnp.dot(
-                jnp.concatenate(pieces, axis=1), weights[:, u].reshape(12 * 128, 128),
+            columns = []
+            for k in range(3):
+                rows = []
+                for (n, m, yi), s in zip(places, chosen):
+                    rows.append(data[g][lax.rem(blocks[k, s, u] + (BLOCKS - 1), BLOCKS), n, m, yi])
+                columns.append(jnp.concatenate(rows, axis=0))
+            every = jnp.dot(
+                jnp.concatenate(columns, axis=1),
+                jnp.concatenate([weights[s, u].reshape(3 * 128, 128) for s in range(4)], axis=1),
                 preferred_element_type=jnp.float32,
-            ).reshape(16, 2, 8, 128)
+            )
+            amplitude = every[:, 3 * 128 :]
+            for s in range(3):
+                amplitude = jnp.where(of_rows == s, every[:, s * 128 : (s + 1) * 128], amplitude)
+            amplitude = amplitude.reshape(16, 2, 8, 128)
             re, im = amplitude[:, 0], amplitude[:, 1]
             pc = gcos[2 * g : 2 * g + 2, :, :, :, lanes].reshape(16, 8, 128).astype(jnp.float32)
             ps = gsin[2 * g : 2 * g + 2, :, :, :, lanes].reshape(16, 8, 128).astype(jnp.float32)
             turned = jnp.concatenate([re * pc - im * ps, re * ps + im * pc], axis=1).reshape(256, 128)
             high = turned.astype(jnp.bfloat16)
-            low = (turned - high.astype(jnp.float32)).astype(jnp.bfloat16)
-            layers = jnp.dot(rotate, high, preferred_element_type=jnp.float32)
-            layers = layers + jnp.dot(rotate, low, preferred_element_type=jnp.float32)
-            vol[slab, :, lanes] += layers[:8] + layers[8:]
+            highs.append(high)
+            lows.append((turned - high.astype(jnp.float32)).astype(jnp.bfloat16))
+        layers = jnp.dot(rotate, jnp.concatenate(highs, axis=1), preferred_element_type=jnp.float32)
+        layers = layers + jnp.dot(rotate, jnp.concatenate(lows, axis=1), preferred_element_type=jnp.float32)
+        vol[slab] += layers[:8] + layers[8:]
 
     complete, far_ready, told = set(), [], []
 
@@ -300,15 +352,15 @@
         elif what == B_DN:
             got(part_b(xm, o, y_dn), ("b_dn", o))
             send(half_b(0, o, y_dn), ("b_far", 0, o), up)
-            send(part_b(xm, o, y_dn), ("b_mate", o, 1), mate)
+            send_mate(part_b(xm, o, y_dn), ("b_mate", o, 1))
         elif what == B_UP:
             got(part_b(xm, o, y_up), ("b_up", o))
             send(half_b(1, o, y_up), ("b_far", 1, o), dn)
-            send(part_b(xm, o, y_up), ("b_mate", o, 2), mate)
+            send_mate(part_b(xm, o, y_up), ("b_mate", o, 2))
         elif what == B_FAR:
             for n in range(2):
                 got(half_b(n, o, y_far), ("b_far", n, o))
-            send(part_b(xm, o, y_far), ("b_mate", o, 3), mate)
+            send_mate(part_b(xm, o, y_far), ("b_mate", o, 3))
         elif what == A_DN:
             got(part_a(o, y_dn), ("a_dn", o))
             send(half_a(0, o, y_dn), ("a_far", 0, o), up)
@@ -321,15 +373,11 @@
             send(data0.at[far_block, 0, xm, y], ("ends_mate",), mate, condition=inner)
         elif what == ENDS_MATE:
             pl.when(inner)(lambda: got(data0.at[far_block, 0, 1 - xm, y], ("ends_mate",)))
-            for d in range(NZ - 1, 0, -1):
-                send(ends(0, y), ("ends_z", d), along[d], ends(d, y), inner)
+            spread_ends(0)
         elif what == ENDS_Z:
-
-            @pl.when(inner)
-            def _():
-                for d in range(1, NZ):
-                    got(ends(d, y), ("ends_z", d))
-
+            pl.when(inner)(lambda: got(ends(o, y), ("ends_z", o)))
+            spread_ends(o)
+        elif what == ENDS_Y:
             for g in range(GROUPS):
                 for n, device in enumerate((up, dn, opposite)):
                     send(ends_all(g, y), ("ends", n, g), device, condition=inner)
@@ -345,7 +393,8 @@
                 pl.semaphore_signal(ready, inc=1, device_id=partner, device_id_type=MESH)
                 told.append(True)
             focus(o, more[0])
-            retire()
+            if o < GROUPS - 1:
+                retire()
             if (o, more[0]) == (GROUPS - 1, 1):
                 give(1, 0, partner)
                 pl.semaphore_wait(ready, 1)
@@ -422,7 +471,7 @@
             pltpu.VMEM((4, 8, NH), f32),
             pltpu.VMEM((NZ, 2, NY, 8, 512), bf16),
             pltpu.VMEM((NZ, 2, NY, 8, 512), bf16),
-            pltpu.VMEM((4, NZ, 2, NY, 16, 128), bf16),
+            pltpu.VMEM((NZ, 2, NY, 16, 128), i32),
             pltpu.VMEM((2, 16, HALF * 16), bf16),
             pltpu.VMEM((2, 8, 512), f32),
             pltpu.VMEM((5, 8, 512), f32),

time: 82.1 us -> 76.9 us (0.937)
  Pallas kernels: 79.3 us -> 74.2 us
    pallas_call x1, Pallas kernels: 79.3 us -> 74.2 us  [local(): pl.pallas_call(kernel, out_shape=jax.ShapeDtypeStruct((2, 4, 512), f32),...]
where the time goes in v4:
time: 76.9 us; the launch traced here: 75.5 us
  Pallas kernels  74.2 us (96%)
  local copies, waits for them, and re-layouts  1.32 us (2%)
    pallas_call x1, Pallas kernels, local(): pl.pallas_call(kernel, out_shape=jax.ShapeDtypeStruct((2, 4, 512), f32),...  74.2 us

profile of v4, /device:TPU:6, one launch (start us, length us, event | category | flops | bytes accessed | tf_op | source)
XLA Modules:
  0.0 75.5 jit_solution(15564894545995159837)
XLA Ops:
  0.0 74.2 %focus.1 = f32[2,4,512]{2,1,0:T(4,128)} custom-call(bf16[2,8,3072]{2,1,0:T(8,128)(2,1)} %bitcast.12, bf16[4,4,3,128,128]{4,3,2,1,0:T(8,128)(2,1)} %bitcast.9, s32[3,4,4]{2,1,0:T(4,128)} %bitcast.15, s32[128]{0:T(128)} %sector_hbm.1, f32[4,8,128]{2,1,0:T(8,128)} %bitcast.13, f32[4,8,128]{2,1,0:T(8,128)} %bitcast.14, bf16[2,2,8,4,8,512]{5,4,3,2,1,0:T(8,128)(2,1)} %bitcast.10, ...), custom_call_target="tpu_custom_call" | custom-call | tf_op jit(solution)/shard_map/focus/pallas_call | solution.py:450
  74.2 1.3 %copy.11 = f32[2,4,512]{2,1,0:T(4,128)} copy(f32[2,4,512]{2,1,0:T(4,128)} %focus.1) | data formatting | bytes 32768

commit v5 on v4

--- a/solution.py
+++ b/solution.py
@@ -322,9 +322,7 @@
 
         send(data[g].at[(WINDOW - 1) * (1 - core)], ("core", g), (h, t + 1 - 2 * core), data[g].at[WINDOW + 1 - core])
 
-    def weights_from_afar():
-        if far_ready:
-            return
+    def tables_from_afar():
         got(cos_far, ("cos",))
         got(sin_far, ("sin",))
         got(blk_far, ("blocks",))
@@ -332,6 +330,10 @@
         copy.start()
         rotation(1, cos_far, sin_far)
         copy.wait()
+
+    def weights_from_afar():
+        if far_ready:
+            return
         for s in range(4):
             got(w_far.at[s], ("weights", s))
         far_ready.append(True)
@@ -381,6 +383,7 @@
             for g in range(GROUPS):
                 for n, device in enumerate((up, dn, opposite)):
                     send(ends_all(g, y), ("ends", n, g), device, condition=inner)
+            tables_from_afar()
         elif what == COMPLETE:
             finish(o)
         elif what == FOCUS:

time: 76.9 us -> 77 us (level)
  no operation moved by 1% of the time
where the time goes in v5:
time: 77 us; the launch traced here: 75.5 us
  Pallas kernels  74.2 us (96%)
  local copies, waits for them, and re-layouts  1.32 us (2%)
    pallas_call x1, Pallas kernels, local(): pl.pallas_call(kernel, out_shape=jax.ShapeDtypeStruct((2, 4, 512), f32),...  74.2 us

profile of v5, /device:TPU:6, one launch (start us, length us, event | category | flops | bytes accessed | tf_op | source)
XLA Modules:
  0.0 75.5 jit_solution(361231970013253916)
XLA Ops:
  0.0 74.2 %focus.1 = f32[2,4,512]{2,1,0:T(4,128)} custom-call(bf16[2,8,3072]{2,1,0:T(8,128)(2,1)} %bitcast.12, bf16[4,4,3,128,128]{4,3,2,1,0:T(8,128)(2,1)} %bitcast.9, s32[3,4,4]{2,1,0:T(4,128)} %bitcast.15, s32[128]{0:T(128)} %sector_hbm.1, f32[4,8,128]{2,1,0:T(8,128)} %bitcast.13, f32[4,8,128]{2,1,0:T(8,128)} %bitcast.14, bf16[2,2,8,4,8,512]{5,4,3,2,1,0:T(8,128)(2,1)} %bitcast.10, ...), custom_call_target="tpu_custom_call" | custom-call | tf_op jit(solution)/shard_map/focus/pallas_call | solution.py:453
  74.2 1.3 %copy.11 = f32[2,4,512]{2,1,0:T(4,128)} copy(f32[2,4,512]{2,1,0:T(4,128)} %focus.1) | data formatting | bytes 32768
